TPU v7x, 768 devices: a whole 4x8x12 slice. The times are simulated.
768 devices in a mesh: leaf: 192 (over z, y, core), sub: 4 (over x).
Axes of the slice: x: 4, y: 8, z: 12, core: 2. Of those that a mesh axis runs over, the one named last changes fastest.
Arguments:
- vectors: float32 [32, 786432], P(None, ('leaf', 'sub')), may hold values from -6 to 6
- bases: float32 [3072, 64, 256], P(('leaf', 'sub')), may hold values from -0.5 to 0.5
- transfers_leaf: float32 [768, 64, 256], P(('leaf', 'sub')), may hold values from -0.5 to 0.5
- transfers_group: float32 [768, 64, 64], P(('leaf', 'sub')), may hold values from -0.75 to 0.75
- near_blocks: float32 [3072, 256, 768], P(('leaf', 'sub')), may hold values from -0.21875 to 0.21875
- near_list: int32 [3072, 3], P(('leaf', 'sub')), may hold values from 0 to 47
- leaf_coupling: float32 [3072, 64, 384], P(('leaf', 'sub')), may hold values from -0.3125 to 0.3125
- leaf_list: int32 [3072, 6], P(('leaf', 'sub')), may hold values from 0 to 47
- leaf_count: int32 [3072], P(('leaf', 'sub')), may hold values from 1 to 6
- coarse_coupling: float32 [192, 64, 1024], P('leaf'), may hold values from -0.1875 to 0.1875
- coarse_list: int32 [192, 16], P('leaf'), may hold values from 0 to 191
- coarse_count: int32 [192], P('leaf'), may hold values from 1 to 16
Outputs:
- product: float32 [32, 786432], P(None, ('leaf', 'sub'))
Inputs may be any that keep to these rules, and one draw needn't show every extreme that they name: `near_list`: the index of a source leaf among the 48 leaves of the group before the target leaf's group, its own group and the group after, in that order. `leaf_list`: the index of a source leaf among the 48 leaves of the group before the target leaf's group, its own group and the group after, in that order; entries at or beyond leaf_count are padding. `coarse_list`: entries at or beyond coarse_count are padding.
All inputs are finite; a program needn't handle non-finite values.
Results may differ from a plain program's by a relative error of at most 0.000068.
Values sent between devices are 32-bit elements; how exact they have to be, the bound alone decides.
A program may use at most 64 MiB of HBM per device.

v0:
```python
import jax
import jax.numpy as jnp
from jax import lax
from jax.sharding import PartitionSpec as P


def padded(block, sides, width):
    for axis, dim in sides:
        count = lax.axis_size(axis)
        forward = [(i, i + 1) for i in range(count - 1)]
        forward.append((count - 1, 0))
        backward = [(target, source) for source, target in forward]
        low = lax.ppermute(
            lax.slice_in_dim(block, block.shape[dim] - width, None, axis=dim), axis, forward
        )
        high = lax.ppermute(lax.slice_in_dim(block, 0, width, axis=dim), axis, backward)
        block = jnp.concatenate([low, block, high], axis=dim)
    return block


def make_pick(targets, usable, divisor, piece):
    owners = jnp.arange(piece.shape[0], dtype=jnp.int32) // divisor
    onehot = ((targets[:, None] == owners[None, :]) & usable[:, None]).astype(jnp.float32)
    return jnp.dot(onehot, piece, precision=lax.Precision.HIGHEST)


def couple_coarse(collected, coupling, slots, rows, rank_size):
    picked = collected.reshape(slots, rows, rank_size)
    return jnp.einsum(
        "krc,akc->ra",
        picked,
        coupling.reshape(rank_size, slots, rank_size),
        precision=lax.Precision.HIGHEST,
    )


def per_device(
    vectors,
    bases,
    transfers_leaf,
    transfers_group,
    near_blocks,
    near_list,
    leaf_coupling,
    leaf_list,
    leaf_count,
    coarse_coupling,
    coarse_list,
    coarse_count,
):
    highest = lax.Precision.HIGHEST
    vec_rows = vectors.shape[0]
    leaves_here = bases.shape[0]
    rank_size = bases.shape[1]
    leaf_points = bases.shape[2]
    near_slots = near_list.shape[1]
    leaf_slots = leaf_list.shape[1]
    coarse_slots = coarse_list.shape[1]
    blocks = vectors.reshape(vec_rows, leaves_here, leaf_points)
    leaf_coef = jnp.einsum("rlp,lap->rla", blocks, bases, precision=highest)
    leaf_flat = leaf_coef.reshape(vec_rows, leaves_here * rank_size)
    device_coef = jnp.einsum("rm,am->ra", leaf_flat, transfers_leaf[0], precision=highest)
    partial_coef = jnp.einsum("rc,ac->ra", device_coef, transfers_group[0], precision=highest)
    entry_width = leaf_points + rank_size
    per_leaf = jnp.concatenate((blocks, leaf_coef), axis=2).reshape(
        vec_rows, 1, leaves_here * entry_width
    )
    grouped = lax.all_gather(per_leaf, "sub", axis=2, tiled=True)
    bordered = padded(grouped, (("leaf", 1),), 1)
    source_table = bordered.reshape(vec_rows, -1, entry_width)
    vector_table = source_table[:, :, :leaf_points]
    coef_table = source_table[:, :, leaf_points:]
    targets = coarse_list[0]
    usable = jnp.arange(coarse_slots, dtype=jnp.int32) < coarse_count[0]
    summed = lax.psum(partial_coef, "sub")
    collected = make_pick(
        targets,
        usable,
        1,
        lax.all_gather(summed.reshape(1, vec_rows * rank_size), "leaf", axis=0, tiled=True),
    )
    coarse_field = couple_coarse(collected, coarse_coupling[0], coarse_slots, vec_rows, rank_size)
    device_field = jnp.einsum("ra,ac->rc", coarse_field, transfers_group[0], precision=highest)
    spread = jnp.einsum("ra,am->rm", device_field, transfers_leaf[0], precision=highest).reshape(
        vec_rows, leaves_here, rank_size
    )
    leaf_mask = (jnp.arange(leaf_slots, dtype=jnp.int32)[None, :] < leaf_count[:, None]).astype(
        jnp.float32
    )
    leaf_picked = coef_table[:, leaf_list] * leaf_mask[None, :, :, None]
    coupled = jnp.einsum(
        "rlkc,lakc->rla",
        leaf_picked,
        leaf_coupling.reshape(leaves_here, rank_size, leaf_slots, rank_size),
        precision=highest,
    )
    leaf_field = coupled + spread
    far_part = jnp.einsum("rla,lap->rlp", leaf_field, bases, precision=highest)
    near_part = jnp.einsum(
        "rlkp,lqkp->rlq",
        vector_table[:, near_list],
        near_blocks.reshape(leaves_here, leaf_points, near_slots, leaf_points),
        precision=highest,
    )
    return (far_part + near_part).reshape(vec_rows, leaves_here * leaf_points)


def solution(mesh):
    return jax.shard_map(
        per_device,
        mesh=mesh,
        in_specs=(
            P(None, ("leaf", "sub")),
            P(("leaf", "sub"), None, None),
            P(("leaf", "sub"), None, None),
            P(("leaf", "sub"), None, None),
            P(("leaf", "sub"), None, None),
            P(("leaf", "sub"), None),
            P(("leaf", "sub"), None, None),
            P(("leaf", "sub"), None),
            P(("leaf", "sub")),
            P("leaf", None, None),
            P("leaf", None),
            P("leaf"),
        ),
        out_specs=P(None, ("leaf", "sub")),
        check_vma=False,
    )
```

profile of v0, /device:TPU:1, one launch (start us, length us, event | category | flops | bytes accessed | tf_op | source)
XLA Modules:
  0.0 157.4 jit_solution(16599201794150100167)
XLA Ops:
  6.5 0.0 copy-start
  6.5 0.0 copy-start.2
  6.6 0.0 all-gather.3.cloned.1.call-start
  6.6 1.1 copy-done
  7.7 1.2 convolution_bitcast_fusion.2
  9.0 0.1 reshape.61
  9.1 1.0 fusion.12
  10.2 0.9 fusion.15
  11.1 0.1 reshape.62
  11.2 10.0 %psum.7 = f32[1,2048]{1,0:T(1,128)} all-reduce(f32[1,2048]{1,0:T(1,128)S(1)} %reshape.62), channel_id=1, replica_groups=mesh['leaf'=192,'sub'=4] {'sub'}, use_global_device_ids=true, to_apply=%region_0.0 | all-reduce | flops 2048 | bytes 16384 | tf_op jit(solution)/shard_map/psum | solution.py:75
  21.2 0.0 all-gather.3.cloned.1.call-update
  21.2 1.0 reshape.57
  22.2 0.3 reshape.58
  22.5 11.4 %all_gather.6 = f32[32,1,5120]{2,1,0:T(1,128)} all-gather(f32[32,1,1280]{2,1,0:T(1,128)S(1)} %reshape.58), channel_id=1, replica_groups=mesh['leaf'=192,'sub'=4] {'sub'}, dimensions={2}, use_global_device_ids=true | all-gather | bytes 819200 | tf_op jit(solution)/shard_map/all_gather | solution.py:68
  33.9 8.4 %collective-permute-start = (f32[32,1,5120]{2,1,0:T(1,128)}, f32[32,1,5120]{2,1,0:T(1,128)}, u32[]{:S(2)}, u32[]{:S(2)}) collective-permute-start(f32[32,1,5120]{2,1,0:T(1,128)} %all_gather.6), channel_id=1, source_target_pairs={{0,4},{4,8},{8,12},{12,16},{16,20},{20,24},{24,28},{28,32},{32,36}... | collective-permute-start | bytes 1966088 | tf_op jit(solution)/shard_map/ppermute | solution.py:13
  42.4 7.1 %collective-permute-start.1 = (f32[32,1,5120]{2,1,0:T(1,128)}, f32[32,1,5120]{2,1,0:T(1,128)}, u32[]{:S(2)}, u32[]{:S(2)}) collective-permute-start(f32[32,1,5120]{2,1,0:T(1,128)} %all_gather.6), channel_id=1, source_target_pairs={{4,0},{8,4},{12,8},{16,12},{20,16},{24,20},{28,24},{32,28},{36,32}... | collective-permute-start | bytes 1966088 | tf_op jit(solution)/shard_map/ppermute | solution.py:16
  49.4 0.0 copy-done.4
  49.5 0.0 copy-done.5
  49.5 0.1 reshape.68
  49.6 0.0 copy-done.1
  49.6 1.2 reshape.60
  51.4 0.0 copy-done.2
  51.4 1.0 reshape_squeeze.3
  52.4 0.0 copy-done.3
  52.4 0.8 copy.38
  53.1 0.1 reshape.76
  53.2 2.4 %copy.32 = f32[4,256,768]{1,2,0:T(8,128)S(1)} copy(f32[4,256,768]{2,1,0:T(8,128)} %param.16) | data formatting | bytes 6291456 | tf_op args[4]
  55.7 0.1 fusion.21
  55.7 0.0 collective-permute-done
  55.8 0.0 collective-permute-done.1
  55.8 4.8 %pad_maximum_fusion = f32[32,3,5120]{2,1,0:T(4,128)} fusion(f32[32,1,5120]{2,1,0:T(1,128)} %collective-permute-done.1, f32[32,1,5120]{2,1,0:T(1,128)} %all_gather.6, f32[32,1,5120]{2,1,0:T(1,128)} %collective-permute-done), kind=kLoop, calls=%fused_computation.2 | loop fusion | flops 983040 | bytes 3932160 | tf_op jit(solution)/shard_map/concatenate | solution.py:17
  60.5 4.4 %reshape.59 = f32[32,48,320]{2,1,0:T(8,128)} reshape(f32[32,3,5120]{2,1,0:T(4,128)} %pad_maximum_fusion) | data formatting | bytes 3932160 | tf_op jit(solution)/shard_map/reshape | solution.py:70
  65.0 1.1 slice-done
  66.1 1.1 copy.40
  67.2 2.1 %copy.41 = f32[32,48,256]{2,0,1:T(8,128)} copy(f32[32,48,256]{2,1,0:T(8,128)S(1)} %slice-done.1) | data formatting | bytes 3145728
  69.3 2.5 %gather_fusion = f32[24,32,64]{2,1,0:T(8,128)} fusion(f32[32,48,64]{2,0,1:T(8,128)} %copy.40, s32[1024]{0:T(1024)S(1)} %pad_clamp_fusion.1), kind=kCustom, calls=%fused_computation | custom fusion | bytes 393312 | tf_op jit(solution)/shard_map/gather | solution.py:90
  71.8 2.7 %gather_fusion.1 = f32[12,32,256]{2,1,0:T(8,128)} fusion(f32[32,48,256]{2,0,1:T(8,128)} %copy.41, s32[1024]{0:T(1024)S(1)} %pad_clamp_fusion), kind=kCustom, calls=%fused_computation.1 | custom fusion | bytes 786480 | tf_op jit(solution)/shard_map/gather | solution.py:101
  74.5 2.9 %convolution_bitcast_fusion.1 = f32[32,4,64]{2,0,1:T(8,128)} fusion(f32[4,64,6,64]{3,2,1,0:T(8,128)} %reshape.60, f32[4,6,32,64]{3,2,1,0:T(8,128)} %bitcast.65, f32[4,6]{1,0:T(4,128)S(1)} %fusion.21), kind=kOutput, calls=%fused_computation.10 | convolution fusion | flops 37797888 | bytes 622688 | tf_op jit(solution)/shard_map/rlkc,lakc->rla/dot_general | solution.py:91
  77.4 62.0 %all-gather.3.cloned.1.call-done = f32[192,1,2048]{2,1,0:T(1,128)} async-done(((f32[1,1,2048]{2,1,0:T(1,128)}), f32[192,1,2048]{2,1,0:T(1,128)}) %all-gather.3.cloned.1.call-update) | async-done | bytes 1572880 | tf_op jit(solution)/shard_map/all_gather | solution.py:80
  139.4 0.0 copy-done.6
  139.4 2.4 %fusion = f32[16,2048]{1,0:T(8,128)S(1)} fusion(f32[192,1,2048]{2,1,0:T(1,128)} %all-gather.3.cloned.1.call-done, s32[16]{0:T(128)S(1)} %bitcast.70, pred[16]{0:T(512)(128)(4,1)S(1)} %iota_compare_fusion.2), kind=kOutput, calls=%fused_computation.3 | convolution fusion | flops 75503616 | bytes 1704016 | tf_op jit(solution)/shard_map/dot_general | solution.py:24
  141.8 0.8 reshape.63
  142.6 1.8 %convolution_bitcast_fusion.4 = f32[32,64]{1,0:T(8,128)S(1)} fusion(f32[16,32,64]{2,1,0:T(8,128)} %reshape.63, f32[64,16,64]{2,1,0:T(8,128)} %reshape_squeeze.3), kind=kOutput, calls=%fused_computation.13 | convolution fusion | flops 25165824 | bytes 401408 | tf_op jit(solution)/shard_map/krc,akc->ra/dot_general | solution.py:29
  144.4 0.9 convolution_bitcast_fusion.3
  145.3 1.4 convolution_add_fusion
  146.7 0.3 fusion.22
  147.0 2.9 %fusion.4 = f32[4,4,8,256]{3,2,1,0:T(8,128)S(1)} fusion(f32[4,32,256]{2,1,0:T(8,128)S(1)} %fusion.22, f32[32,4,3,256]{3,0,2,1:T(8,128)} %bitcast.64, f32[4,256,3,256]{1,3,2,0:T(8,128)S(1)} %bitcast.63), kind=kOutput, calls=%fused_computation.8 | convolution fusion | flops 302022656 | bytes 3801088 | tf_op jit(solution)/shard_map/rlkp,lqkp->rlq/dot_general | solution.py:99
  149.9 0.7 copy.43
  (17 shorter events, 0.1 us)
Async XLA Ops:
  6.5 1.2 copy-start
  6.5 45.9 %copy-start.3 = (f32[1,64,256]{2,1,0:T(8,128)S(1)}, f32[1,64,256]{2,1,0:T(8,128)}, u32[]{:S(2)}) copy-start(f32[1,64,256]{2,1,0:T(8,128)} %param.14) | copy-start | bytes 196612
  6.5 42.9 %copy-start.4 = (s32[4,6]{1,0:T(4,128)S(1)}, s32[4,6]{1,0:T(4,128)}, u32[]{:S(2)}) copy-start(s32[4,6]{1,0:T(4,128)} %param.19) | copy-start | bytes 292
  6.5 42.9 %copy-start.5 = (s32[4,3]{1,0:T(4,128)S(1)}, s32[4,3]{1,0:T(4,128)}, u32[]{:S(2)}) copy-start(s32[4,3]{1,0:T(4,128)} %param.17) | copy-start | bytes 148
  6.5 43.0 %copy-start.1 = (f32[4,64,384]{2,1,0:T(8,128)S(1)}, f32[4,64,384]{2,1,0:T(8,128)}, u32[]{:S(2)}) copy-start(f32[4,64,384]{2,1,0:T(8,128)} %param.18) | copy-start | bytes 1179652
  6.5 44.9 %copy-start.2 = (f32[1,64,1024]{2,1,0:T(8,128)S(1)}, f32[1,64,1024]{2,1,0:T(8,128)}, u32[]{:S(2)}) copy-start(f32[1,64,1024]{2,1,0:T(8,128)} %param.21) | copy-start | bytes 786436
  6.6 132.8 %all-gather.3.cloned.1.call-start = ((), (), s32[]{:S(2)}) async-start(), calls=%async_computation | async-start | bytes 1581056 | tf_op jit(solution)/shard_map/all_gather | solution.py:80
  33.9 21.8 %collective-permute-start = (f32[32,1,5120]{2,1,0:T(1,128)}, f32[32,1,5120]{2,1,0:T(1,128)}, u32[]{:S(2)}, u32[]{:S(2)}) collective-permute-start(f32[32,1,5120]{2,1,0:T(1,128)} %all_gather.6), channel_id=1, source_target_pairs={{0,4},{4,8},{8,12},{12,16},{16,20},{20,24},{24,28},{28,32},{32,36}... | collective-permute-start | bytes 1966088 | tf_op jit(solution)/shard_map/ppermute | solution.py:13
  42.4 13.4 %collective-permute-start.1 = (f32[32,1,5120]{2,1,0:T(1,128)}, f32[32,1,5120]{2,1,0:T(1,128)}, u32[]{:S(2)}, u32[]{:S(2)}) collective-permute-start(f32[32,1,5120]{2,1,0:T(1,128)} %all_gather.6), channel_id=1, source_target_pairs={{4,0},{8,4},{12,8},{16,12},{20,16},{24,20},{28,24},{32,28},{36,32}... | collective-permute-start | bytes 1966088 | tf_op jit(solution)/shard_map/ppermute | solution.py:16
  53.2 2.4 %copy-start.7 = (s32[4]{0:T(128)S(1)}, s32[4]{0:T(128)}, u32[]{:S(2)}) copy-start(s32[4]{0:T(128)} %param.20) | copy-start | bytes 52
  65.0 1.1 slice-start
  65.0 2.3 %slice-start.1 = ((f32[32,48,320]{2,1,0:T(8,128)}), f32[32,48,256]{2,1,0:T(8,128)S(1)}, s32[]{:S(2)}) async-start(f32[32,48,320]{2,1,0:T(8,128)} %reshape.59), calls=%async_computation.2 | async-start | bytes 3145728 | tf_op jit(solution)/shard_map/slice | solution.py:71
  67.2 72.1 %copy-start.6 = (s32[1,16]{1,0:T(1,128)S(1)}, s32[1,16]{1,0:T(1,128)}, u32[]{:S(2)}) copy-start(s32[1,16]{1,0:T(1,128)} %param.22) | copy-start | bytes 196
Sparse Core Ops, SparseCore 0:
  21.3 118.0 all-gather.2
where the time goes:
time: 158 us; the launch traced here: 157 us
  waiting for transfers between devices  62 us (39%)
  local copies, waits for them, and re-layouts  23.5 us (15%)
  blocking collectives  21.4 us (14%)
  matrix products  15.7 us (10%)
  starting transfers between devices  15.5 us (10%)
  between operations  14.3 us (9%)
  other arithmetic  4.93 us (3%)
    all_gather x1, waiting for transfers between devices, per_device(): lax.all_gather(summed.reshape(1, vec_rows * rank_size), 'leaf', axis=0, t...  62 us
    all_gather x1, blocking collectives, per_device(): grouped = lax.all_gather(per_leaf, 'sub', axis=2, tiled=True)  11.4 us
    psum x1, blocking collectives, per_device(): summed = lax.psum(partial_coef, 'sub')  9.99 us
    ppermute x1, starting transfers between devices, padded(): lax.ppermute(lax.slice_in_dim(block, block.shape[dim] - width, None, axis...  8.41 us
    ppermute x1, starting transfers between devices, padded(): lax.ppermute(lax.slice_in_dim(block, 0, width, axis=dim), axis, backward)  7.08 us
    unnamed x19, local copies, waits for them, and re-layouts  6.73 us
    concatenate x1, other arithmetic, padded(): block = jnp.concatenate([low, block, high], axis=dim)  4.79 us
    reshape x1, local copies, waits for them, and re-layouts, per_device(): source_table = bordered.reshape(vec_rows, -1, entry_width)  4.43 us
  transfers between devices with their start and end apart: 3, of which 1 were waited for; matrix products, arithmetic and copies ran while one was open for 17% of the time, Pallas kernels for 0%

commit v1 on v0

v1 whole, which is shorter than its diff:
```python
import functools

import jax
import jax.numpy as jnp
from jax import lax
from jax.experimental import pallas as pl
from jax.experimental.pallas import tpu as pltpu
from jax.sharding import PartitionSpec as P

F32 = jnp.float32
BF16 = jnp.bfloat16
MESH = pl.DeviceIdType.MESH
ROWS = 32
PTS = 256
RANK = 64
SUBS = 4
CORES = 2
NY = 8
NZ = 12
KA = 6
NEAR = 3
K2 = 16
X_ORDER = (1, 3, 2)


def split(a):
    high = a.astype(BF16)
    return high, (a - high.astype(F32)).astype(BF16)


def dot(a, b, dim):
    return lax.dot_general(a, b, (((1,), (dim,)), ((), ())), preferred_element_type=F32)


def mul(a, b, dim):
    a_high, a_low = split(a)
    b_high, b_low = split(b)
    return dot(a_high, b_high, dim) + (dot(a_high, b_low, dim) + dot(a_low, b_high, dim))


def kernel(
    near_list,
    leaf_list,
    leaf_count,
    coarse_list,
    coarse_count,
    x_hbm,
    bases_hbm,
    tl_hbm,
    tg_hbm,
    near_hbm,
    la_hbm,
    ca_hbm,
    out_ref,
    xtab,
    ctab,
    bases,
    tl,
    tg,
    near,
    la,
    ca,
    mfold,
    pre,
    stage,
    rs_in,
    col,
    table,
    cf_stage,
    cf_all,
    load_sem,
    x_send,
    x_recv,
    rs_send,
    rs_recv,
    y_send,
    y_recv,
    z_send,
    z_recv,
    cf_send,
    cf_recv,
):
    leaf = lax.axis_index("leaf")
    s = lax.axis_index("sub")
    c = lax.rem(leaf, 2)
    y = lax.rem(lax.div(leaf, 2), NY)
    z = lax.div(leaf, 2 * NY)

    def leaf_of(zz, yy, cc):
        return zz * (2 * NY) + yy * 2 + cc

    def sub_at(d):
        return lax.rem(s + d, SUBS)

    sibling = leaf_of(z, y, 1 - c)
    partner = lax.rem(leaf + 192 + 2 * c - 1, 192)
    y_devs = [(leaf_of(z, lax.rem(y + d, NY), c), s) for d in range(1, NY)]

    loads = []

    def load(src, dst):
        cp = pltpu.make_async_copy(src, dst, load_sem.at[len(loads)])
        cp.start()
        loads.append(cp)
        return cp

    own = (SUBS + s) * 4
    x_loads = [
        load(x_hbm.at[:, pl.ds(j * PTS, PTS)], xtab.at[own + j]) for j in range(4)
    ]
    b_load = load(bases_hbm, bases)
    tl_load = load(tl_hbm, tl)
    tg_load = load(tg_hbm, tg)
    ca_load = load(ca_hbm, ca)
    la_load = load(la_hbm, la)
    near_load = load(near_hbm, near)

    barrier = pltpu.get_barrier_semaphore()
    met = 0

    def greet(dev):
        pl.semaphore_signal(barrier, inc=1, device_id=dev, device_id_type=MESH)

    for d in range(SUBS):
        for cc in range(2):
            if d == 0 and cc == 0:
                continue
            greet((leaf if cc == 0 else sibling, sub_at(d)))
            met += 1
    greet((partner, s))
    met += 1
    for dev in y_devs:
        greet(dev)
        met += 1
    for d in range(1, NZ):
        for cc in range(2):
            greet((leaf_of(lax.rem(z + d, NZ), y, c if cc == 0 else 1 - c), s))
            met += 1

    for cp in x_loads:
        cp.wait()
    b_load.wait()
    pairs = []
    for h in range(2):
        a0 = mul(xtab[own + 2 * h], bases[2 * h], 1)
        a1 = mul(xtab[own + 2 * h + 1], bases[2 * h + 1], 1)
        pairs.append(jnp.concatenate([a0, a1], axis=1))
    c_own = (SUBS + s) * 2
    for h in range(2):
        ctab[c_own + h] = pairs[h]
    tl_load.wait()
    tg_load.wait()
    fold = mul(tg[0], tl[0], 0)
    partial = mul(jnp.concatenate(pairs, axis=1), fold, 1)
    zero = jnp.zeros_like(partial)
    here = jnp.where(
        c == 0,
        jnp.concatenate([partial, zero], axis=1),
        jnp.concatenate([zero, partial], axis=1),
    )
    stage[...] = here.reshape(SUBS, 8, 128)

    pl.semaphore_wait(barrier, met)

    def remote(src, dst, send, recv, dev):
        return pltpu.make_async_remote_copy(
            src_ref=src,
            dst_ref=dst,
            send_sem=send,
            recv_sem=recv,
            device_id=dev,
            device_id_type=MESH,
        )

    sent = []

    def push(*args):
        cp = remote(*args)
        cp.start()
        sent.append(cp)
        return cp

    rs = []
    for d in range(SUBS):
        for cc in range(2):
            if d == 0 and cc == 0:
                continue
            to = sub_at(d)
            rs.append(
                push(
                    stage.at[to],
                    rs_in.at[d, cc],
                    rs_send.at[d, cc],
                    rs_recv.at[d, cc],
                    (leaf if cc == 0 else sibling, to),
                )
            )

    to_sibling = 2 * c
    to_partner = 2 - 2 * c

    def x_part(group, sub):
        return xtab.at[pl.ds((group * SUBS + sub) * 4, 4)]

    def c_part(group, sub):
        return ctab.at[pl.ds((group * SUBS + sub) * 2, 2)]

    def spread_block(d, sub):
        for i, part in enumerate((x_part, c_part)):
            push(part(1, sub), part(to_partner, sub), x_send.at[i, 2, d], x_recv.at[i, 2, d], (partner, s))
            push(part(1, sub), part(to_sibling, sub), x_send.at[i, 1, d], x_recv.at[i, 1, d], (sibling, s))

    for i, part in enumerate((x_part, c_part)):
        for d in X_ORDER:
            push(part(1, s), part(1, s), x_send.at[i, 0, d], x_recv.at[i, 0, d], (leaf, sub_at(d)))
    spread_block(0, s)

    for cp in rs:
        cp.wait_recv()
    tile = stage[s]
    for d in range(SUBS):
        for cc in range(2):
            if d == 0 and cc == 0:
                continue
            tile = tile + rs_in[d, cc]
    col[y] = tile
    ys = [
        push(col.at[y], col.at[y], y_send.at[i], y_recv.at[i], dev)
        for i, dev in enumerate(y_devs)
    ]

    for j in range(4):
        mfold[:, j * PTS : (j + 1) * PTS] = mul(fold[:, j * RANK : (j + 1) * RANK], bases[j], 0)

    for i in range(NY - 1):
        slot = col.at[lax.rem(y + NY - 1 - i, NY)]
        remote(slot, slot, y_send.at[i], y_recv.at[i], y_devs[i]).wait_recv()
    half = pl.ds(c * 4, 4)
    for d in range(1, NZ):
        for cc in range(2):
            push(
                col.at[half],
                table.at[z, half],
                z_send.at[d, cc],
                z_recv.at[d, cc],
                (leaf_of(lax.rem(z + d, NZ), y, c if cc == 0 else 1 - c), s),
            )
    table[z] = col[...]

    def arrived(i, way, d, ref):
        remote(ref, ref, x_send.at[i, way, d], x_recv.at[i, way, d], (sibling, s)).wait_recv()

    for d in X_ORDER:
        sub = lax.rem(s + SUBS - d, SUBS)
        arrived(0, 0, d, x_part(1, sub))
        arrived(1, 0, d, c_part(1, sub))
        spread_block(d, sub)
    for d in range(SUBS):
        sub = lax.rem(s + SUBS - d, SUBS)
        for i, part in enumerate((x_part, c_part)):
            arrived(i, 1, d, part(2 - 2 * c, sub))
            arrived(i, 2, d, part(2 * c, sub))

    lane = lax.broadcasted_iota(jnp.int32, (ROWS, 128), 1)

    def picked(tab, entry, k, use):
        both = tab[lax.div(entry, 2)]
        turned = pltpu.roll(both, 64, 1)
        keep = jnp.where(lax.rem(entry, 2) == k % 2, 1.0, 0.0) * use
        turn = use - keep
        return both * keep + turned * turn

    la_load.wait()
    near_load.wait()
    for j in range(4):
        pieces = []
        for k in range(0, KA, 2):
            lo, hi = (
                picked(ctab, leaf_list[j, q], q, jnp.where(q < leaf_count[j], 1.0, 0.0))
                for q in (k, k + 1)
            )
            pieces.append(jnp.where(lane < RANK, lo, hi))
        coupled = mul(jnp.concatenate(pieces, axis=1), la[j], 1)
        far = mul(coupled, bases[j], 0)
        sources = jnp.concatenate([xtab[near_list[j, k]] for k in range(NEAR)], axis=1)
        pre[:, j * PTS : (j + 1) * PTS] = far + mul(sources, near[j], 1)

    for d in range(1, NZ):
        zz = lax.rem(z + NZ - d, NZ)
        for cc in range(2):
            part = table.at[zz, pl.ds((c if cc == 0 else 1 - c) * 4, 4)]
            remote(part, part, z_send.at[d, cc], z_recv.at[d, cc], (sibling, s)).wait_recv()
    ca_load.wait()
    lane8 = lax.broadcasted_iota(jnp.int32, (8, 128), 1)
    pieces = []
    for k in range(0, K2, 2):
        two = []
        for q in (k, k + 1):
            entry = coarse_list[0, q]
            chip = lax.div(entry, 2)
            both = table[lax.div(chip, NY), lax.rem(chip, NY)]
            turned = pltpu.roll(both, 64, 1)
            use = jnp.where(q < coarse_count[0], 1.0, 0.0)
            keep = jnp.where(lax.rem(entry, 2) == q % 2, 1.0, 0.0) * use
            two.append(both * keep + turned * (use - keep))
        pieces.append(jnp.where(lane8 < RANK, two[0], two[1]))
    field = mul(jnp.concatenate(pieces, axis=1), ca[0], 1)
    cf_all[s] = jnp.concatenate([field, jnp.zeros_like(field)], axis=1)
    cfs = [
        push(cf_all.at[s], cf_all.at[s], cf_send.at[d], cf_recv.at[d], (leaf, sub_at(d)))
        for d in range(1, SUBS)
    ]
    for d in range(1, SUBS):
        slot = cf_all.at[lax.rem(s + SUBS - d, SUBS)]
        remote(slot, slot, cf_send.at[d], cf_recv.at[d], (sibling, s)).wait_recv()
    field_all = cf_all[...].reshape(ROWS, 128)[:, :RANK]
    out_ref[...] = pre[...] + mul(field_all, mfold[...], 0)

    for cp in sent:
        cp.wait_send()


def per_device(
    vectors,
    bases,
    transfers_leaf,
    transfers_group,
    near_blocks,
    near_list,
    leaf_coupling,
    leaf_list,
    leaf_count,
    coarse_coupling,
    coarse_list,
    coarse_count,
):
    smem = pl.BlockSpec(memory_space=pltpu.SMEM)
    anywhere = pl.BlockSpec(memory_space=pl.ANY)
    dma = pltpu.SemaphoreType.DMA
    return pl.pallas_call(
        kernel,
        out_shape=jax.ShapeDtypeStruct(vectors.shape, F32),
        in_specs=[smem] * 5 + [anywhere] * 7,
        out_specs=pl.BlockSpec(memory_space=pltpu.VMEM),
        scratch_shapes=[
            pltpu.VMEM((48, ROWS, PTS), F32),
            pltpu.VMEM((24, ROWS, 128), F32),
            pltpu.VMEM(bases.shape, F32),
            pltpu.VMEM(transfers_leaf.shape, F32),
            pltpu.VMEM(transfers_group.shape, F32),
            pltpu.VMEM(near_blocks.shape, F32),
            pltpu.VMEM(leaf_coupling.shape, F32),
            pltpu.VMEM(coarse_coupling.shape, F32),
            pltpu.VMEM((RANK, 4 * PTS), F32),
            pltpu.VMEM((ROWS, 4 * PTS), F32),
            pltpu.VMEM((SUBS, 8, 128), F32),
            pltpu.VMEM((SUBS, 2, 8, 128), F32),
            pltpu.VMEM((NY, 8, 128), F32),
            pltpu.VMEM((NZ, NY, 8, 128), F32),
            pltpu.VMEM((8, 128), F32),
            pltpu.VMEM((SUBS, 8, 128), F32),
            dma((10,)),
            dma((2, 3, SUBS)),
            dma((2, 3, SUBS)),
            dma((SUBS, 2)),
            dma((SUBS, 2)),
            dma((NY - 1,)),
            dma((NY - 1,)),
            dma((NZ, 2)),
            dma((NZ, 2)),
            dma((SUBS,)),
            dma((SUBS,)),
        ],
        compiler_params=pltpu.CompilerParams(
            collective_id=0, has_side_effects=True, vmem_limit_bytes=40 * 1024 * 1024
        ),
    )(
        near_list,
        leaf_list,
        leaf_count,
        coarse_list,
        coarse_count,
        vectors,
        bases,
        transfers_leaf,
        transfers_group,
        near_blocks,
        leaf_coupling,
        coarse_coupling,
    )


def solution(mesh):
    return jax.shard_map(
        per_device,
        mesh=mesh,
        in_specs=(
            P(None, ("leaf", "sub")),
            P(("leaf", "sub"), None, None),
            P(("leaf", "sub"), None, None),
            P(("leaf", "sub"), None, None),
            P(("leaf", "sub"), None, None),
            P(("leaf", "sub"), None),
            P(("leaf", "sub"), None, None),
            P(("leaf", "sub"), None),
            P(("leaf", "sub")),
            P("leaf", None, None),
            P("leaf", None),
            P("leaf"),
        ),
        out_specs=P(None, ("leaf", "sub")),
        check_vma=False,
    )
```

time: 158 us -> 66.1 us (0.42)
  the two profiles are of different devices: /device:TPU:1 before, /device:TPU:4 now
where the time goes in v1:
time: 66.1 us; the launch traced here: 65.6 us
  Pallas kernels  54.4 us (82%)
  local copies, waits for them, and re-layouts  10.6 us (16%)
  between operations  0.68 us (1%)
    pallas_call x1, Pallas kernels, per_device(): pl.pallas_call(kernel, out_shape=jax.ShapeDtypeStruct(vectors.shape, F32)...  54.4 us
    unnamed x23, local copies, waits for them, and re-layouts  10.6 us

profile of v1, /device:TPU:4, one launch (start us, length us, event | category | flops | bytes accessed | tf_op | source)
XLA Modules:
  0.0 65.6 jit_solution(3850833498806822596)
XLA Ops:
  0.7 0.0 copy-start
  0.7 1.9 %copy-done = f32[4,256,768]{2,1,0:T(8,128)S(1)} copy-done((f32[4,256,768]{2,1,0:T(8,128)S(1)}, f32[4,256,768]{2,1,0:T(8,128)}, u32[]{:S(2)}) %copy-start) | copy-done | bytes 3145752
  2.5 0.0 copy-start.1
  2.5 1.0 %copy-done.1 = f32[4,64,384]{2,1,0:T(8,128)S(1)} copy-done((f32[4,64,384]{2,1,0:T(8,128)S(1)}, f32[4,64,384]{2,1,0:T(8,128)}, u32[]{:S(2)}) %copy-start.1) | copy-done | bytes 393240
  3.5 0.0 copy-start.2
  3.5 0.9 %copy-done.2 = f32[4,64,256]{2,1,0:T(8,128)S(1)} copy-done((f32[4,64,256]{2,1,0:T(8,128)S(1)}, f32[4,64,256]{2,1,0:T(8,128)}, u32[]{:S(2)}) %copy-start.2) | copy-done | bytes 262168
  4.5 0.0 copy-start.3
  4.5 0.9 %copy-done.3 = f32[1,64,1024]{2,1,0:T(8,128)S(1)} copy-done((f32[1,64,1024]{2,1,0:T(8,128)S(1)}, f32[1,64,1024]{2,1,0:T(8,128)}, u32[]{:S(2)}) %copy-start.3) | copy-done | bytes 262168
  5.4 0.0 copy-start.4
  5.4 0.9 %copy-done.4 = f32[32,1024]{1,0:T(8,128)S(1)} copy-done((f32[32,1024]{1,0:T(8,128)S(1)}, f32[32,1024]{1,0:T(8,128)}, u32[]{:S(2)}) %copy-start.4) | copy-done | bytes 131096
  6.3 0.0 copy-start.5
  6.3 0.8 %copy-done.5 = f32[1,64,256]{2,1,0:T(8,128)S(1)} copy-done((f32[1,64,256]{2,1,0:T(8,128)S(1)}, f32[1,64,256]{2,1,0:T(8,128)}, u32[]{:S(2)}) %copy-start.5) | copy-done | bytes 65560
  7.2 0.0 copy-start.6
  7.2 0.8 %copy-done.6 = f32[1,64,64]{2,1,0:T(8,128)S(1)} copy-done((f32[1,64,64]{2,1,0:T(8,128)S(1)}, f32[1,64,64]{2,1,0:T(8,128)}, u32[]{:S(2)}) %copy-start.6) | copy-done | bytes 16408
  7.9 0.0 copy-start.7
  7.9 0.7 %copy-done.7 = s32[4,3]{1,0:T(4,128)S(1)} copy-done((s32[4,3]{1,0:T(4,128)S(1)}, s32[4,3]{1,0:T(4,128)}, u32[]{:S(2)}) %copy-start.7) | copy-done | bytes 72
  8.6 0.0 copy-start.8
  8.6 0.7 %copy-done.8 = s32[4,6]{1,0:T(4,128)S(1)} copy-done((s32[4,6]{1,0:T(4,128)S(1)}, s32[4,6]{1,0:T(4,128)}, u32[]{:S(2)}) %copy-start.8) | copy-done | bytes 120
  9.3 0.0 copy-start.9
  9.3 0.7 copy-done.9
  10.0 0.0 copy-start.10
  10.0 0.7 copy-done.10
  10.6 54.4 %shard_map.118 = f32[32,1024]{1,0:T(8,128)S(1)} custom-call(s32[4,3]{1,0:T(4,128)S(1)} %copy-done.7, s32[4,6]{1,0:T(4,128)S(1)} %copy-done.8, s32[4]{0:T(128)S(1)} %copy-done.9, s32[1,16]{1,0:T(1,128)S(1)} %copy-done.10, s32[1]{0:T(128)S(6)} %copy.14.coarse_count, f32[32,1024]{1,0:T(8,128)S(1)} %copy-done.4, f32[4,64,256]{2,1,0:T(8,128)S(1)} %copy-done.2, ...), custom_call_target="tpu_custom_call" | custom-call | tf_op jit(solution)/shard_map/pallas_call | solution.py:340
  65.0 0.7 %copy.15 = f32[32,1024]{1,0:T(8,128)} copy(f32[32,1024]{1,0:T(8,128)S(1)} %shard_map.118) | data formatting | bytes 262144
Async XLA Ops:
  0.7 1.9 %copy-start = (f32[4,256,768]{2,1,0:T(8,128)S(1)}, f32[4,256,768]{2,1,0:T(8,128)}, u32[]{:S(2)}) copy-start(f32[4,256,768]{2,1,0:T(8,128)} %near_hbm.1) | copy-start | bytes 9437188
  2.5 1.0 %copy-start.1 = (f32[4,64,384]{2,1,0:T(8,128)S(1)}, f32[4,64,384]{2,1,0:T(8,128)}, u32[]{:S(2)}) copy-start(f32[4,64,384]{2,1,0:T(8,128)} %la_hbm.1) | copy-start | bytes 1179652
  3.5 0.9 %copy-start.2 = (f32[4,64,256]{2,1,0:T(8,128)S(1)}, f32[4,64,256]{2,1,0:T(8,128)}, u32[]{:S(2)}) copy-start(f32[4,64,256]{2,1,0:T(8,128)} %bases_hbm.1) | copy-start | bytes 786436
  4.5 0.9 %copy-start.3 = (f32[1,64,1024]{2,1,0:T(8,128)S(1)}, f32[1,64,1024]{2,1,0:T(8,128)}, u32[]{:S(2)}) copy-start(f32[1,64,1024]{2,1,0:T(8,128)} %ca_hbm.1) | copy-start | bytes 786436
  5.4 0.9 %copy-start.4 = (f32[32,1024]{1,0:T(8,128)S(1)}, f32[32,1024]{1,0:T(8,128)}, u32[]{:S(2)}) copy-start(f32[32,1024]{1,0:T(8,128)} %x_hbm.1) | copy-start | bytes 393220
  6.3 0.8 %copy-start.5 = (f32[1,64,256]{2,1,0:T(8,128)S(1)}, f32[1,64,256]{2,1,0:T(8,128)}, u32[]{:S(2)}) copy-start(f32[1,64,256]{2,1,0:T(8,128)} %tl_hbm.1) | copy-start | bytes 196612
  7.2 0.8 %copy-start.6 = (f32[1,64,64]{2,1,0:T(8,128)S(1)}, f32[1,64,64]{2,1,0:T(8,128)}, u32[]{:S(2)}) copy-start(f32[1,64,64]{2,1,0:T(8,128)} %tg_hbm.1) | copy-start | bytes 49156
  7.9 0.7 %copy-start.7 = (s32[4,3]{1,0:T(4,128)S(1)}, s32[4,3]{1,0:T(4,128)}, u32[]{:S(2)}) copy-start(s32[4,3]{1,0:T(4,128)} %near_list.1) | copy-start | bytes 148
  8.6 0.7 %copy-start.8 = (s32[4,6]{1,0:T(4,128)S(1)}, s32[4,6]{1,0:T(4,128)}, u32[]{:S(2)}) copy-start(s32[4,6]{1,0:T(4,128)} %leaf_list.1) | copy-start | bytes 292
  9.3 0.7 copy-start.9
  10.0 0.7 copy-start.10

commit v2 on v1

v2 whole, which is shorter than its diff:
```python
import functools

import jax
import jax.numpy as jnp
from jax import lax
from jax.experimental import pallas as pl
from jax.experimental.pallas import tpu as pltpu
from jax.sharding import PartitionSpec as P

F32 = jnp.float32
BF16 = jnp.bfloat16
MESH = pl.DeviceIdType.MESH
ROWS = 32
PTS = 256
RANK = 64
SUBS = 4
CORES = 2
NY = 8
NZ = 12
KA = 6
NEAR = 3
K2 = 16
X_ORDER = (1, 3, 2)


def split(a):
    high = a.astype(BF16)
    return high, (a - high.astype(F32)).astype(BF16)


def dot(a, b, dim):
    return lax.dot_general(a, b, (((1,), (dim,)), ((), ())), preferred_element_type=F32)


def mul(a, b, dim):
    a_high, a_low = split(a)
    b_high, b_low = split(b)
    return dot(a_high, b_high, dim) + (dot(a_high, b_low, dim) + dot(a_low, b_high, dim))


def kernel(
    near_list_hbm,
    leaf_list_hbm,
    leaf_count_hbm,
    coarse_list_hbm,
    coarse_count_hbm,
    x_hbm,
    bases_hbm,
    tl_hbm,
    tg_hbm,
    near_hbm,
    la_hbm,
    ca_hbm,
    out_ref,
    near_list,
    leaf_list,
    leaf_count,
    coarse_list,
    coarse_count,
    xtab,
    ctab,
    bases,
    tl,
    tg,
    near,
    la,
    ca,
    mfold,
    pre,
    stage,
    rs_in,
    mine,
    table,
    cf_all,
    load_sem,
    x_send,
    x_recv,
    rs_send,
    rs_recv,
    z_send,
    z_recv,
    s_send,
    s_recv,
    cf_send,
    cf_recv,
):
    leaf = lax.axis_index("leaf")
    s = lax.axis_index("sub")
    c = lax.rem(leaf, 2)
    y = lax.rem(lax.div(leaf, 2), NY)
    z = lax.div(leaf, 2 * NY)

    def leaf_of(zz, yy, cc):
        return zz * (2 * NY) + yy * 2 + cc

    def sub_at(d):
        return lax.rem(s + d, SUBS)

    sibling = leaf_of(z, y, 1 - c)
    partner = lax.rem(leaf + 192 + 2 * c - 1, 192)
    row = [(d, cc) for d in range(SUBS) for cc in range(CORES) if d + cc]

    def row_dev(d, cc):
        return (sibling if cc else leaf, sub_at(d))

    def plane_dev(i, dy):
        return (leaf_of(lax.rem(z + 2 * i + c, NZ), lax.rem(y + dy, NY), c), s)

    def far_first(pair):
        i, dy = pair
        z_hops = min(2 * i, NZ - 2 * i) + min(2 * i + 1, NZ - 2 * i - 1)
        return -(z_hops / 2 + min(dy, NY - dy))

    plane = sorted(
        ((i, dy) for i in range(NZ // 2) for dy in range(NY) if i + dy), key=far_first
    )

    loads = {}

    def load(name, src, dst):
        loads[name] = pltpu.make_async_copy(src, dst, load_sem.at[len(loads)])
        loads[name].start()

    own = (SUBS + s) * 4
    for j in range(4):
        load("x%d" % j, x_hbm.at[:, pl.ds(j * PTS, PTS)], xtab.at[own + j])
    load("bases", bases_hbm, bases)
    load("tl", tl_hbm, tl)
    load("tg", tg_hbm, tg)

    barrier = pltpu.get_barrier_semaphore()

    def greet(dev):
        pl.semaphore_signal(barrier, inc=1, device_id=dev, device_id_type=MESH)

    def back(i, dy):
        return (leaf_of(lax.rem(z + NZ - 2 * i - c, NZ), lax.rem(y + NY - dy, NY), c), s)

    for d, cc in row:
        greet(row_dev(d, cc))
    greet((partner, s))
    for i, dy in plane:
        greet(back(i, dy))

    @pl.when(c == 1)
    def _():
        greet(back(0, 0))

    for j in range(4):
        loads["x%d" % j].wait()
    loads["bases"].wait()
    pairs = []
    for h in range(2):
        a0 = mul(xtab[own + 2 * h], bases[2 * h], 1)
        a1 = mul(xtab[own + 2 * h + 1], bases[2 * h + 1], 1)
        pairs.append(jnp.concatenate([a0, a1], axis=1))
    c_own = (SUBS + s) * 2
    for h in range(2):
        ctab[c_own + h] = pairs[h]
    loads["tl"].wait()
    loads["tg"].wait()
    fold = mul(tg[0], tl[0], 0)
    partial = mul(jnp.concatenate(pairs, axis=1), fold, 1)
    zero = jnp.zeros_like(partial)
    here = jnp.where(
        c == 0,
        jnp.concatenate([partial, zero], axis=1),
        jnp.concatenate([zero, partial], axis=1),
    )
    stage[...] = here.reshape(SUBS, 8, 128)

    pl.semaphore_wait(barrier, len(row) + 1 + len(plane) + c)

    def remote(src, dst, send, recv, dev):
        return pltpu.make_async_remote_copy(
            src_ref=src,
            dst_ref=dst,
            send_sem=send,
            recv_sem=recv,
            device_id=dev,
            device_id_type=MESH,
        )

    sent = []

    def push(*args):
        cp = remote(*args)
        cp.start()
        sent.append(cp)
        return cp

    rs = [
        push(
            stage.at[sub_at(d)],
            rs_in.at[d, cc],
            rs_send.at[d, cc],
            rs_recv.at[d, cc],
            row_dev(d, cc),
        )
        for d, cc in row
    ]

    to_sibling = 2 * c
    to_partner = 2 - 2 * c

    def x_part(group, sub):
        return xtab.at[pl.ds((group * SUBS + sub) * 4, 4)]

    def c_part(group, sub):
        return ctab.at[pl.ds((group * SUBS + sub) * 2, 2)]

    def spread_block(d, sub):
        for i, part in enumerate((x_part, c_part)):
            push(part(1, sub), part(to_partner, sub), x_send.at[i, 2, d], x_recv.at[i, 2, d], (partner, s))
            push(part(1, sub), part(to_sibling, sub), x_send.at[i, 1, d], x_recv.at[i, 1, d], (sibling, s))

    for i, part in enumerate((x_part, c_part)):
        for d in X_ORDER:
            push(part(1, s), part(1, s), x_send.at[i, 0, d], x_recv.at[i, 0, d], (leaf, sub_at(d)))
    spread_block(0, s)

    load("ca", ca_hbm, ca)
    load("la", la_hbm, la)
    load("near", near_hbm, near)
    lists = (
        (near_list_hbm, near_list),
        (leaf_list_hbm, leaf_list),
        (leaf_count_hbm, leaf_count),
        (coarse_list_hbm, coarse_list),
        (coarse_count_hbm, coarse_count),
    )
    for i, (src, dst) in enumerate(lists):
        load("list%d" % i, src, dst)

    for cp in rs:
        cp.wait_recv()
    tile = stage[s]
    for d, cc in row:
        tile = tile + rs_in[d, cc]
    mine[...] = tile

    @pl.when(c == 0)
    def _():
        table[z, y] = tile

    for i, dy in plane:
        remote(mine, table.at[z, y], z_send.at[i], z_recv.at[i], plane_dev(i, dy)).start()

    @pl.when(c == 1)
    def _():
        remote(mine, table.at[z, y], z_send.at[0], z_recv.at[0], plane_dev(0, 0)).start()

    for j in range(4):
        mfold[:, j * PTS : (j + 1) * PTS] = mul(fold[:, j * RANK : (j + 1) * RANK], bases[j], 0)

    def arrived(i, way, d, ref):
        remote(ref, ref, x_send.at[i, way, d], x_recv.at[i, way, d], (sibling, s)).wait_recv()

    for d in X_ORDER:
        sub = lax.rem(s + SUBS - d, SUBS)
        arrived(0, 0, d, x_part(1, sub))
        arrived(1, 0, d, c_part(1, sub))
        spread_block(d, sub)

    def tiles_in(i, count):
        ref = table.at[0, pl.ds(0, count)]
        return remote(ref, ref, z_send.at[i], z_recv.at[i], (sibling, s))

    def own_tiles(wait):
        @pl.when(c == 1)
        def _():
            wait(tiles_in(0, NY))

        @pl.when(c == 0)
        def _():
            wait(tiles_in(0, NY - 1))

    for i in (0, 5, 1, 4, 2, 3):
        if i:
            tiles_in(i, NY).wait_recv()
        else:
            own_tiles(lambda cp: cp.wait_recv())
        part = table.at[lax.rem(z + NZ - 2 * i - c, NZ)]
        push(part, part, s_send.at[i], s_recv.at[i], (sibling, s))

    for i in range(len(lists)):
        loads["list%d" % i].wait()
    loads["ca"].wait()
    for i in range(NZ // 2):
        part = table.at[lax.rem(z + NZ - 2 * i - 1 + c, NZ)]
        remote(part, part, s_send.at[i], s_recv.at[i], (sibling, s)).wait_recv()
    lane8 = lax.broadcasted_iota(jnp.int32, (8, 128), 1)
    pieces = []
    for k in range(0, K2, 2):
        two = []
        for q in (k, k + 1):
            entry = coarse_list[0, q]
            chip = lax.div(entry, 2)
            both = table[lax.div(chip, NY), lax.rem(chip, NY)]
            turned = pltpu.roll(both, 64, 1)
            use = jnp.where(q < coarse_count[0], 1.0, 0.0)
            keep = jnp.where(lax.rem(entry, 2) == q % 2, 1.0, 0.0) * use
            two.append(both * keep + turned * (use - keep))
        pieces.append(jnp.where(lane8 < RANK, two[0], two[1]))
    field = mul(jnp.concatenate(pieces, axis=1), ca[0], 1)
    cf_all[s] = jnp.concatenate([field, jnp.zeros_like(field)], axis=1)
    for d in range(1, SUBS):
        push(cf_all.at[s], cf_all.at[s], cf_send.at[d], cf_recv.at[d], (leaf, sub_at(d)))

    for d in range(SUBS):
        sub = lax.rem(s + SUBS - d, SUBS)
        for i, part in enumerate((x_part, c_part)):
            arrived(i, 1, d, part(2 - 2 * c, sub))
            arrived(i, 2, d, part(2 * c, sub))
    lane = lax.broadcasted_iota(jnp.int32, (ROWS, 128), 1)

    def picked(entry, k, use):
        both = ctab[lax.div(entry, 2)]
        turned = pltpu.roll(both, 64, 1)
        keep = jnp.where(lax.rem(entry, 2) == k % 2, 1.0, 0.0) * use
        return both * keep + turned * (use - keep)

    loads["la"].wait()
    loads["near"].wait()
    for j in range(4):
        pieces = []
        for k in range(0, KA, 2):
            lo, hi = (
                picked(leaf_list[j, q], q, jnp.where(q < leaf_count[j], 1.0, 0.0))
                for q in (k, k + 1)
            )
            pieces.append(jnp.where(lane < RANK, lo, hi))
        coupled = mul(jnp.concatenate(pieces, axis=1), la[j], 1)
        far = mul(coupled, bases[j], 0)
        sources = jnp.concatenate([xtab[near_list[j, k]] for k in range(NEAR)], axis=1)
        pre[:, j * PTS : (j + 1) * PTS] = far + mul(sources, near[j], 1)

    for d in range(1, SUBS):
        slot = cf_all.at[lax.rem(s + SUBS - d, SUBS)]
        remote(slot, slot, cf_send.at[d], cf_recv.at[d], (sibling, s)).wait_recv()
    field_all = cf_all[...].reshape(ROWS, 128)[:, :RANK]
    out_ref[...] = pre[...] + mul(field_all, mfold[...], 0)

    for cp in sent:
        cp.wait_send()
    for i in range(1, NZ // 2):
        tiles_in(i, NY).wait_send()
    own_tiles(lambda cp: cp.wait_send())


def per_device(
    vectors,
    bases,
    transfers_leaf,
    transfers_group,
    near_blocks,
    near_list,
    leaf_coupling,
    leaf_list,
    leaf_count,
    coarse_coupling,
    coarse_list,
    coarse_count,
):
    in_hbm = pl.BlockSpec(memory_space=pltpu.HBM)
    dma = pltpu.SemaphoreType.DMA
    return pl.pallas_call(
        kernel,
        out_shape=jax.ShapeDtypeStruct(vectors.shape, F32),
        in_specs=[in_hbm] * 12,
        out_specs=pl.BlockSpec(memory_space=pltpu.VMEM),
        scratch_shapes=[
            pltpu.SMEM(near_list.shape, jnp.int32),
            pltpu.SMEM(leaf_list.shape, jnp.int32),
            pltpu.SMEM(leaf_count.shape, jnp.int32),
            pltpu.SMEM(coarse_list.shape, jnp.int32),
            pltpu.SMEM(coarse_count.shape, jnp.int32),
            pltpu.VMEM((48, ROWS, PTS), F32),
            pltpu.VMEM((24, ROWS, 128), F32),
            pltpu.VMEM(bases.shape, F32),
            pltpu.VMEM(transfers_leaf.shape, F32),
            pltpu.VMEM(transfers_group.shape, F32),
            pltpu.VMEM(near_blocks.shape, F32),
            pltpu.VMEM(leaf_coupling.shape, F32),
            pltpu.VMEM(coarse_coupling.shape, F32),
            pltpu.VMEM((RANK, 4 * PTS), F32),
            pltpu.VMEM((ROWS, 4 * PTS), F32),
            pltpu.VMEM((SUBS, 8, 128), F32),
            pltpu.VMEM((SUBS, 2, 8, 128), F32),
            pltpu.VMEM((8, 128), F32),
            pltpu.VMEM((NZ, NY, 8, 128), F32),
            pltpu.VMEM((SUBS, 8, 128), F32),
            dma((15,)),
            dma((2, 3, SUBS)),
            dma((2, 3, SUBS)),
            dma((SUBS, 2)),
            dma((SUBS, 2)),
            dma((NZ // 2,)),
            dma((NZ // 2,)),
            dma((NZ // 2,)),
            dma((NZ // 2,)),
            dma((SUBS,)),
            dma((SUBS,)),
        ],
        compiler_params=pltpu.CompilerParams(
            collective_id=0, has_side_effects=True, vmem_limit_bytes=60 * 1024 * 1024
        ),
    )(
        near_list,
        leaf_list,
        leaf_count,
        coarse_list,
        coarse_count,
        vectors,
        bases,
        transfers_leaf,
        transfers_group,
        near_blocks,
        leaf_coupling,
        coarse_coupling,
    )


def solution(mesh):
    return jax.shard_map(
        per_device,
        mesh=mesh,
        in_specs=(
            P(None, ("leaf", "sub")),
            P(("leaf", "sub"), None, None),
            P(("leaf", "sub"), None, None),
            P(("leaf", "sub"), None, None),
            P(("leaf", "sub"), None, None),
            P(("leaf", "sub"), None),
            P(("leaf", "sub"), None, None),
            P(("leaf", "sub"), None),
            P(("leaf", "sub")),
            P("leaf", None, None),
            P("leaf", None),
            P("leaf"),
        ),
        out_specs=P(None, ("leaf", "sub")),
        check_vma=False,
    )
```

time: 66.1 us -> 45.3 us (0.69)
  the two profiles are of different devices: /device:TPU:4 before, /device:TPU:1 now
where the time goes in v2:
time: 45.3 us; the launch traced here: 45.2 us
  Pallas kernels  42.9 us (95%)
  local copies, waits for them, and re-layouts  1.57 us (3%)
  between operations  0.66 us (1%)
    pallas_call x1, Pallas kernels, per_device(): pl.pallas_call(kernel, out_shape=jax.ShapeDtypeStruct(vectors.shape, F32)...  42.9 us
    unnamed x1, local copies, waits for them, and re-layouts  1.57 us

profile of v2, /device:TPU:1, one launch (start us, length us, event | category | flops | bytes accessed | tf_op | source)
XLA Modules:
  0.0 45.2 jit_solution(14453250878127749916)
XLA Ops:
  0.7 42.9 %shard_map.118 = f32[32,1024]{1,0:T(8,128)} custom-call(s32[4,3]{1,0:T(4,128)} %near_list_hbm.1, s32[4,6]{1,0:T(4,128)} %leaf_list_hbm.1, s32[4]{0:T(128)} %leaf_count_hbm.1, s32[1,16]{1,0:T(1,128)} %coarse_list_hbm.1, s32[1]{0:T(128)S(6)} %copy.14.coarse_count_hbm, f32[32,1024]{1,0:T(8,128)} %x_hbm.1, f32[4,64,256]{2,1,0:T(8,128)} %bases_hbm.1, ...), custom_call_target="tpu_custom_call" | custom-call | tf_op jit(solution)/shard_map/pallas_call | solution.py:367
  43.6 1.6 %copy.15 = f32[32,1024]{1,0:T(8,128)} copy(f32[32,1024]{1,0:T(8,128)} %shard_map.118) | data formatting | bytes 262144

commit v3 on v2

--- a/solution.py
+++ b/solution.py
@@ -21,6 +21,7 @@
 NEAR = 3
 K2 = 16
 X_ORDER = (1, 3, 2)
+DYS = (4, 3, 5, 2, 6, 1, 7)
 
 
 def split(a):
@@ -72,6 +73,7 @@
     mine,
     table,
     cf_all,
+    seen,
     load_sem,
     x_send,
     x_recv,
@@ -103,17 +105,11 @@
     def row_dev(d, cc):
         return (sibling if cc else leaf, sub_at(d))
 
-    def plane_dev(i, dy):
-        return (leaf_of(lax.rem(z + 2 * i + c, NZ), lax.rem(y + dy, NY), c), s)
-
-    def far_first(pair):
-        i, dy = pair
-        z_hops = min(2 * i, NZ - 2 * i) + min(2 * i + 1, NZ - 2 * i - 1)
-        return -(z_hops / 2 + min(dy, NY - dy))
-
-    plane = sorted(
-        ((i, dy) for i in range(NZ // 2) for dy in range(NY) if i + dy), key=far_first
-    )
+    def plane_dev(p, dy):
+        return (leaf_of(p, lax.rem(y + dy, NY), c), s)
+
+    first = lax.rem(z + c, 2)
+    below = lax.div(z + c, 2)
 
     loads = {}
 
@@ -133,18 +129,21 @@
     def greet(dev):
         pl.semaphore_signal(barrier, inc=1, device_id=dev, device_id_type=MESH)
 
-    def back(i, dy):
-        return (leaf_of(lax.rem(z + NZ - 2 * i - c, NZ), lax.rem(y + NY - dy, NY), c), s)
-
     for d, cc in row:
         greet(row_dev(d, cc))
     greet((partner, s))
-    for i, dy in plane:
-        greet(back(i, dy))
-
-    @pl.when(c == 1)
+
+    @pl.when(c == 0)
     def _():
-        greet(back(0, 0))
+        for dy in range(1, NY):
+            greet(plane_dev(z, dy))
+
+    def greet_plane(q, carry):
+        for dy in range(NY):
+            greet(plane_dev(first + 2 * q, dy))
+        return carry
+
+    lax.fori_loop(below + 1 - c, NZ // 2, greet_plane, 0)
 
     for j in range(4):
         loads["x%d" % j].wait()
@@ -169,7 +168,7 @@
     )
     stage[...] = here.reshape(SUBS, 8, 128)
 
-    pl.semaphore_wait(barrier, len(row) + 1 + len(plane) + c)
+    pl.semaphore_wait(barrier, len(row) + 1 + (1 - c) * (NY - 1) + below * NY)
 
     def remote(src, dst, send, recv, dev):
         return pltpu.make_async_remote_copy(
@@ -218,6 +217,18 @@
         for d in X_ORDER:
             push(part(1, s), part(1, s), x_send.at[i, 0, d], x_recv.at[i, 0, d], (leaf, sub_at(d)))
     spread_block(0, s)
+
+    def tell_plane(q, carry):
+        for dy in range(NY):
+            pl.semaphore_signal(
+                seen.at[lax.div(z, 2)],
+                inc=1,
+                device_id=plane_dev(first + 2 * q, dy),
+                device_id_type=MESH,
+            )
+        return carry
+
+    lax.fori_loop(0, below, tell_plane, 0)
 
     load("ca", ca_hbm, ca)
     load("la", la_hbm, la)
@@ -243,12 +254,20 @@
     def _():
         table[z, y] = tile
 
-    for i, dy in plane:
-        remote(mine, table.at[z, y], z_send.at[i], z_recv.at[i], plane_dev(i, dy)).start()
-
-    @pl.when(c == 1)
+    def tile_to(p, dys):
+        half = lax.div(p, 2)
+        for dy in dys:
+            remote(mine, table.at[z, y], z_send.at[half], z_recv.at[lax.div(z, 2)], plane_dev(p, dy)).start()
+
+    def tile_below(q, carry):
+        tile_to(first + 2 * q, DYS + (0,))
+        return carry
+
+    lax.fori_loop(0, below, tile_below, 0)
+
+    @pl.when(c == 0)
     def _():
-        remote(mine, table.at[z, y], z_send.at[0], z_recv.at[0], plane_dev(0, 0)).start()
+        tile_to(z, DYS)
 
     for j in range(4):
         mfold[:, j * PTS : (j + 1) * PTS] = mul(fold[:, j * RANK : (j + 1) * RANK], bases[j], 0)
@@ -262,32 +281,43 @@
         arrived(1, 0, d, c_part(1, sub))
         spread_block(d, sub)
 
-    def tiles_in(i, count):
+    def tiles_at(p, count):
         ref = table.at[0, pl.ds(0, count)]
-        return remote(ref, ref, z_send.at[i], z_recv.at[i], (sibling, s))
-
-    def own_tiles(wait):
-        @pl.when(c == 1)
-        def _():
-            wait(tiles_in(0, NY))
-
+        half = lax.div(p, 2)
+        return remote(ref, ref, z_send.at[half], z_recv.at[half], (sibling, s))
+
+    def own_plane(wait):
         @pl.when(c == 0)
         def _():
-            wait(tiles_in(0, NY - 1))
-
-    for i in (0, 5, 1, 4, 2, 3):
+            wait(tiles_at(z, NY - 1))
+
+    for i in range(NZ // 2):
+        p = z + 2 * i + c
+
+        @pl.when((p > z) & (p < NZ))
+        def _():
+            pl.semaphore_wait(seen.at[lax.div(p, 2)], NY)
+            tile_to(p, DYS + (0,))
+
+    for i in range(NZ // 2):
+        p = lax.rem(z + 2 * i + c, NZ)
         if i:
-            tiles_in(i, NY).wait_recv()
+            tiles_at(p, NY).wait_recv()
         else:
-            own_tiles(lambda cp: cp.wait_recv())
-        part = table.at[lax.rem(z + NZ - 2 * i - c, NZ)]
+            own_plane(lambda cp: cp.wait_recv())
+
+            @pl.when(c == 1)
+            def _():
+                tiles_at(p, NY).wait_recv()
+
+        part = table.at[p]
         push(part, part, s_send.at[i], s_recv.at[i], (sibling, s))
 
     for i in range(len(lists)):
         loads["list%d" % i].wait()
     loads["ca"].wait()
     for i in range(NZ // 2):
-        part = table.at[lax.rem(z + NZ - 2 * i - 1 + c, NZ)]
+        part = table.at[lax.rem(z + 2 * i + 1 - c, NZ)]
         remote(part, part, s_send.at[i], s_recv.at[i], (sibling, s)).wait_recv()
     lane8 = lax.broadcasted_iota(jnp.int32, (8, 128), 1)
     pieces = []
@@ -343,9 +373,15 @@
 
     for cp in sent:
         cp.wait_send()
-    for i in range(1, NZ // 2):
-        tiles_in(i, NY).wait_send()
-    own_tiles(lambda cp: cp.wait_send())
+    for i in range(NZ // 2):
+        if i:
+            tiles_at(lax.rem(z + 2 * i + c, NZ), NY).wait_send()
+        else:
+            own_plane(lambda cp: cp.wait_send())
+
+            @pl.when(c == 1)
+            def _():
+                tiles_at(lax.rem(z + 1, NZ), NY).wait_send()
 
 
 def per_device(
@@ -390,6 +426,7 @@
             pltpu.VMEM((8, 128), F32),
             pltpu.VMEM((NZ, NY, 8, 128), F32),
             pltpu.VMEM((SUBS, 8, 128), F32),
+            pltpu.SemaphoreType.REGULAR((NZ // 2,)),
             dma((15,)),
             dma((2, 3, SUBS)),
             dma((2, 3, SUBS)),

time: 45.3 us -> 42.6 us (0.940)
  the two profiles are of different devices: /device:TPU:1 before, /device:TPU:2 now
where the time goes in v3:
time: 42.6 us; the launch traced here: 42.4 us
  Pallas kernels  40.2 us (94%)
  local copies, waits for them, and re-layouts  1.57 us (4%)
  between operations  0.66 us (2%)
    pallas_call x1, Pallas kernels, per_device(): pl.pallas_call(kernel, out_shape=jax.ShapeDtypeStruct(vectors.shape, F32)...  40.2 us
    unnamed x1, local copies, waits for them, and re-layouts  1.57 us

profile of v3, /device:TPU:2, one launch (start us, length us, event | category | flops | bytes accessed | tf_op | source)
XLA Modules:
  0.0 42.4 jit_solution(6399180762850460288)
XLA Ops:
  0.7 40.2 %shard_map.118 = f32[32,1024]{1,0:T(8,128)} custom-call(s32[4,3]{1,0:T(4,128)} %near_list_hbm.1, s32[4,6]{1,0:T(4,128)} %leaf_list_hbm.1, s32[4]{0:T(128)} %leaf_count_hbm.1, s32[1,16]{1,0:T(1,128)} %coarse_list_hbm.1, s32[1]{0:T(128)S(6)} %copy.14.coarse_count_hbm, f32[32,1024]{1,0:T(8,128)} %x_hbm.1, f32[4,64,256]{2,1,0:T(8,128)} %bases_hbm.1, ...), custom_call_target="tpu_custom_call" | custom-call | tf_op jit(solution)/shard_map/pallas_call | solution.py:403
  40.8 1.6 %copy.15 = f32[32,1024]{1,0:T(8,128)} copy(f32[32,1024]{1,0:T(8,128)} %shard_map.118) | data formatting | bytes 262144

commit v4 on v3

--- a/solution.py
+++ b/solution.py
@@ -199,24 +199,25 @@
         for d, cc in row
     ]
 
-    to_sibling = 2 * c
-    to_partner = 2 - 2 * c
-
     def x_part(group, sub):
         return xtab.at[pl.ds((group * SUBS + sub) * 4, 4)]
 
     def c_part(group, sub):
         return ctab.at[pl.ds((group * SUBS + sub) * 2, 2)]
 
-    def spread_block(d, sub):
+    def to_sibling(d, sub):
         for i, part in enumerate((x_part, c_part)):
-            push(part(1, sub), part(to_partner, sub), x_send.at[i, 2, d], x_recv.at[i, 2, d], (partner, s))
-            push(part(1, sub), part(to_sibling, sub), x_send.at[i, 1, d], x_recv.at[i, 1, d], (sibling, s))
+            push(part(1, sub), part(2 * c, sub), x_send.at[i, 1, d], x_recv.at[i, 1, d], (sibling, s))
+
+    def to_row(way, group):
+        for i, part in enumerate((x_part, c_part)):
+            for d in X_ORDER:
+                push(part(group, s), part(group, s), x_send.at[i, way, d], x_recv.at[i, way, d], (leaf, sub_at(d)))
 
     for i, part in enumerate((x_part, c_part)):
-        for d in X_ORDER:
-            push(part(1, s), part(1, s), x_send.at[i, 0, d], x_recv.at[i, 0, d], (leaf, sub_at(d)))
-    spread_block(0, s)
+        push(part(1, s), part(2 - 2 * c, s), x_send.at[i, 2, 0], x_recv.at[i, 2, 0], (partner, s))
+    to_row(0, 1)
+    to_sibling(0, s)
 
     def tell_plane(q, carry):
         for dy in range(NY):
@@ -279,7 +280,10 @@
         sub = lax.rem(s + SUBS - d, SUBS)
         arrived(0, 0, d, x_part(1, sub))
         arrived(1, 0, d, c_part(1, sub))
-        spread_block(d, sub)
+        to_sibling(d, sub)
+    arrived(0, 2, 0, x_part(2 * c, s))
+    arrived(1, 2, 0, c_part(2 * c, s))
+    to_row(2, 2 * c)
 
     def tiles_at(p, count):
         ref = table.at[0, pl.ds(0, count)]
@@ -341,7 +345,8 @@
         sub = lax.rem(s + SUBS - d, SUBS)
         for i, part in enumerate((x_part, c_part)):
             arrived(i, 1, d, part(2 - 2 * c, sub))
-            arrived(i, 2, d, part(2 * c, sub))
+            if d:
+                arrived(i, 2, d, part(2 * c, sub))
     lane = lax.broadcasted_iota(jnp.int32, (ROWS, 128), 1)
 
     def picked(entry, k, use):
@@ -398,6 +403,7 @@
     coarse_list,
     coarse_count,
 ):
+    stay = functools.partial(pltpu.with_memory_space_constraint, memory_space=pltpu.HBM)
     in_hbm = pl.BlockSpec(memory_space=pltpu.HBM)
     dma = pltpu.SemaphoreType.DMA
     return pl.pallas_call(
@@ -440,21 +446,21 @@
             dma((SUBS,)),
         ],
         compiler_params=pltpu.CompilerParams(
-            collective_id=0, has_side_effects=True, vmem_limit_bytes=60 * 1024 * 1024
+            collective_id=0, has_side_effects=True, vmem_limit_bytes=32 * 1024 * 1024
         ),
     )(
-        near_list,
-        leaf_list,
-        leaf_count,
-        coarse_list,
+        stay(near_list),
+        stay(leaf_list),
+        stay(leaf_count),
+        stay(coarse_list),
         coarse_count,
-        vectors,
-        bases,
-        transfers_leaf,
-        transfers_group,
-        near_blocks,
-        leaf_coupling,
-        coarse_coupling,
+        stay(vectors),
+        stay(bases),
+        stay(transfers_leaf),
+        stay(transfers_group),
+        stay(near_blocks),
+        stay(leaf_coupling),
+        stay(coarse_coupling),
     )
 
 

time: 42.6 us -> 37.4 us (0.88)
  the two profiles are of different devices: /device:TPU:2 before, /device:TPU:1 now
where the time goes in v4:
time: 37.4 us; the launch traced here: 37.2 us
  Pallas kernels  35.9 us (96%)
  local copies, waits for them, and re-layouts  0.66 us (2%)
  between operations  0.66 us (2%)
    pallas_call x1, Pallas kernels, per_device(): pl.pallas_call(kernel, out_shape=jax.ShapeDtypeStruct(vectors.shape, F32)...  35.9 us

profile of v4, /device:TPU:1, one launch (start us, length us, event | category | flops | bytes accessed | tf_op | source)
XLA Modules:
  0.0 37.2 jit_solution(13144357711636778901)
XLA Ops:
  0.7 35.9 %shard_map.118 = f32[32,1024]{1,0:T(8,128)S(1)} custom-call(s32[4,3]{1,0:T(4,128)} %near_list_hbm.1, s32[4,6]{1,0:T(4,128)} %leaf_list_hbm.1, s32[4]{0:T(128)} %leaf_count_hbm.1, s32[1,16]{1,0:T(1,128)} %coarse_list_hbm.1, s32[1]{0:T(128)S(6)} %copy.14.coarse_count_hbm, f32[32,1024]{1,0:T(8,128)} %x_hbm.1, f32[4,64,256]{2,1,0:T(8,128)} %bases_hbm.1, ...), custom_call_target="tpu_custom_call" | custom-call | tf_op jit(solution)/shard_map/pallas_call | solution.py:409
  36.5 0.7 %copy.15 = f32[32,1024]{1,0:T(8,128)} copy(f32[32,1024]{1,0:T(8,128)S(1)} %shard_map.118) | data formatting | bytes 262144

commit v5 on v4

--- a/solution.py
+++ b/solution.py
@@ -21,7 +21,8 @@
 NEAR = 3
 K2 = 16
 X_ORDER = (1, 3, 2)
-DYS = (4, 3, 5, 2, 6, 1, 7)
+YS = (0, 1, 7, 2, 6, 3, 5, 4)
+LATE = 10
 
 
 def split(a):
@@ -37,6 +38,13 @@
     a_high, a_low = split(a)
     b_high, b_low = split(b)
     return dot(a_high, b_high, dim) + (dot(a_high, b_low, dim) + dot(a_low, b_high, dim))
+
+
+def mul_parts(a, b_high, b_low, dim):
+    rows = a.shape[0]
+    a_high, a_low = split(a)
+    both = dot(jnp.concatenate([a_high, a_low], axis=0), b_high, dim)
+    return both[:rows] + (dot(a_high, b_low, dim) + both[rows:])
 
 
 def kernel(
@@ -52,7 +60,9 @@
     near_hbm,
     la_hbm,
     ca_hbm,
-    out_ref,
+    pre,
+    m_ref,
+    field_ref,
     near_list,
     leaf_list,
     leaf_count,
@@ -66,13 +76,19 @@
     near,
     la,
     ca,
-    mfold,
-    pre,
+    near_high,
+    near_low,
+    ca_high,
+    ca_low,
     stage,
     rs_in,
     mine,
     table,
-    cf_all,
+    cf_out,
+    cf_in,
+    sib_ca,
+    sib_list,
+    sib_count,
     seen,
     load_sem,
     x_send,
@@ -206,18 +222,48 @@
         return ctab.at[pl.ds((group * SUBS + sub) * 2, 2)]
 
     def to_sibling(d, sub):
-        for i, part in enumerate((x_part, c_part)):
-            push(part(1, sub), part(2 * c, sub), x_send.at[i, 1, d], x_recv.at[i, 1, d], (sibling, s))
+        return [
+            remote(part(1, sub), part(2 * c, sub), x_send.at[i, 1, d], x_recv.at[i, 1, d], (sibling, s))
+            for i, part in enumerate((x_part, c_part))
+        ]
 
     def to_row(way, group):
-        for i, part in enumerate((x_part, c_part)):
-            for d in X_ORDER:
-                push(part(group, s), part(group, s), x_send.at[i, way, d], x_recv.at[i, way, d], (leaf, sub_at(d)))
+        return [
+            remote(part(group, s), part(group, s), x_send.at[i, way, d], x_recv.at[i, way, d], (leaf, sub_at(d)))
+            for i, part in enumerate((x_part, c_part))
+            for d in X_ORDER
+        ]
+
+    def arrived(i, way, d, ref):
+        remote(ref, ref, x_send.at[i, way, d], x_recv.at[i, way, d], (sibling, s)).wait_recv()
+
+    def start_all(cps):
+        for cp in cps:
+            cp.start()
 
     for i, part in enumerate((x_part, c_part)):
         push(part(1, s), part(2 - 2 * c, s), x_send.at[i, 2, 0], x_recv.at[i, 2, 0], (partner, s))
-    to_row(0, 1)
-    to_sibling(0, s)
+    own_block = to_row(0, 1) + to_sibling(0, s)
+    row_blocks = [(d, to_sibling(d, lax.rem(s + SUBS - d, SUBS))) for d in X_ORDER]
+    partner_block = to_row(2, 2 * c)
+    for cps in [own_block, partner_block] + [cps for _, cps in row_blocks]:
+        sent.extend(cps)
+
+    def hand_on():
+        arrived(0, 2, 0, x_part(2 * c, s))
+        arrived(1, 2, 0, c_part(2 * c, s))
+        start_all(partner_block)
+        for d, cps in row_blocks:
+            sub = lax.rem(s + SUBS - d, SUBS)
+            arrived(0, 0, d, x_part(1, sub))
+            arrived(1, 0, d, c_part(1, sub))
+            start_all(cps)
+
+    late = z >= LATE
+
+    @pl.when(jnp.logical_not(late))
+    def _():
+        start_all(own_block)
 
     def tell_plane(q, carry):
         for dy in range(NY):
@@ -255,35 +301,69 @@
     def _():
         table[z, y] = tile
 
-    def tile_to(p, dys):
-        half = lax.div(p, 2)
-        for dy in dys:
-            remote(mine, table.at[z, y], z_send.at[half], z_recv.at[lax.div(z, 2)], plane_dev(p, dy)).start()
+    def tile_to(dev, half):
+        remote(mine, table.at[z, y], z_send.at[half], z_recv.at[lax.div(z, 2)], dev).start()
+
+    def tile_to_plane(p):
+        for yy in YS:
+            tile_to((leaf_of(p, yy, c), s), lax.div(p, 2))
 
     def tile_below(q, carry):
-        tile_to(first + 2 * q, DYS + (0,))
+        tile_to_plane(first + 2 * q)
         return carry
 
     lax.fori_loop(0, below, tile_below, 0)
 
     @pl.when(c == 0)
     def _():
-        tile_to(z, DYS)
+        for dy in range(1, NY):
+            tile_to(plane_dev(z, dy), lax.div(z, 2))
 
     for j in range(4):
-        mfold[:, j * PTS : (j + 1) * PTS] = mul(fold[:, j * RANK : (j + 1) * RANK], bases[j], 0)
-
-    def arrived(i, way, d, ref):
-        remote(ref, ref, x_send.at[i, way, d], x_recv.at[i, way, d], (sibling, s)).wait_recv()
-
-    for d in X_ORDER:
-        sub = lax.rem(s + SUBS - d, SUBS)
-        arrived(0, 0, d, x_part(1, sub))
-        arrived(1, 0, d, c_part(1, sub))
-        to_sibling(d, sub)
-    arrived(0, 2, 0, x_part(2 * c, s))
-    arrived(1, 2, 0, c_part(2 * c, s))
-    to_row(2, 2 * c)
+        piece = mul(fold[:, j * RANK : (j + 1) * RANK], bases[j], 0)
+        m_ref[:, j * PTS : (j + 1) * PTS] = piece
+
+    @pl.when(jnp.logical_not(late))
+    def _():
+        hand_on()
+
+    for name in ("near", "la", "ca"):
+        loads[name].wait()
+    for i in range(len(lists)):
+        loads["list%d" % i].wait()
+    for j in range(4):
+        near_high[j], near_low[j] = split(near[j])
+    shared = ((ca, sib_ca), (coarse_list, sib_list), (coarse_count, sib_count))
+    for i, (src, dst) in enumerate(shared):
+        push(src, dst, s_send.at[i], s_recv.at[i], (sibling, s))
+
+    def near_field():
+        for d in range(SUBS):
+            sub = lax.rem(s + SUBS - d, SUBS)
+            for i, part in enumerate((x_part, c_part)):
+                arrived(i, 1, d, part(2 - 2 * c, sub))
+                if d:
+                    arrived(i, 2, d, part(2 * c, sub))
+        lane = lax.broadcasted_iota(jnp.int32, (ROWS, 128), 1)
+
+        def picked(entry, k, use):
+            both = ctab[lax.div(entry, 2)]
+            turned = pltpu.roll(both, 64, 1)
+            keep = jnp.where(lax.rem(entry, 2) == k % 2, 1.0, 0.0) * use
+            return both * keep + turned * (use - keep)
+
+        for j in range(4):
+            pieces = []
+            for k in range(0, KA, 2):
+                lo, hi = (
+                    picked(leaf_list[j, q], q, jnp.where(q < leaf_count[j], 1.0, 0.0))
+                    for q in (k, k + 1)
+                )
+                pieces.append(jnp.where(lane < RANK, lo, hi))
+            coupled = mul(jnp.concatenate(pieces, axis=1), la[j], 1)
+            far = mul(coupled, bases[j], 0)
+            sources = jnp.concatenate([xtab[near_list[j, k]] for k in range(NEAR)], axis=1)
+            pre[:, j * PTS : (j + 1) * PTS] = far + mul_parts(sources, near_high[j], near_low[j], 1)
 
     def tiles_at(p, count):
         ref = table.at[0, pl.ds(0, count)]
@@ -301,7 +381,32 @@
         @pl.when((p > z) & (p < NZ))
         def _():
             pl.semaphore_wait(seen.at[lax.div(p, 2)], NY)
-            tile_to(p, DYS + (0,))
+            tile_to_plane(p)
+
+    @pl.when(late)
+    def _():
+        start_all(own_block)
+        hand_on()
+
+    near_last = late | (leaf == 0)
+
+    @pl.when(jnp.logical_not(near_last))
+    def _():
+        near_field()
+
+    for i, (_, dst) in enumerate(shared):
+        remote(dst, dst, s_send.at[i], s_recv.at[i], (sibling, s)).wait_recv()
+    ca_high[...], ca_low[...] = split(jnp.concatenate([ca[0], sib_ca[0]], axis=0))
+    picked_tiles = []
+    for entries, count in ((coarse_list, coarse_count), (sib_list, sib_count)):
+        picks = []
+        for q in range(K2):
+            entry = entries[0, q]
+            chip = lax.div(entry, 2)
+            plane = lax.div(chip, NY)
+            use = (q < count[0]) & (lax.rem(plane + z, 2) == c)
+            picks.append((plane, lax.rem(chip, NY), lax.rem(entry, 2) == q % 2, use))
+        picked_tiles.append(picks)
 
     for i in range(NZ // 2):
         p = lax.rem(z + 2 * i + c, NZ)
@@ -314,67 +419,38 @@
             def _():
                 tiles_at(p, NY).wait_recv()
 
-        part = table.at[p]
-        push(part, part, s_send.at[i], s_recv.at[i], (sibling, s))
-
-    for i in range(len(lists)):
-        loads["list%d" % i].wait()
-    loads["ca"].wait()
-    for i in range(NZ // 2):
-        part = table.at[lax.rem(z + 2 * i + 1 - c, NZ)]
-        remote(part, part, s_send.at[i], s_recv.at[i], (sibling, s)).wait_recv()
     lane8 = lax.broadcasted_iota(jnp.int32, (8, 128), 1)
-    pieces = []
-    for k in range(0, K2, 2):
-        two = []
-        for q in (k, k + 1):
-            entry = coarse_list[0, q]
-            chip = lax.div(entry, 2)
-            both = table[lax.div(chip, NY), lax.rem(chip, NY)]
-            turned = pltpu.roll(both, 64, 1)
-            use = jnp.where(q < coarse_count[0], 1.0, 0.0)
-            keep = jnp.where(lax.rem(entry, 2) == q % 2, 1.0, 0.0) * use
-            two.append(both * keep + turned * (use - keep))
-        pieces.append(jnp.where(lane8 < RANK, two[0], two[1]))
-    field = mul(jnp.concatenate(pieces, axis=1), ca[0], 1)
-    cf_all[s] = jnp.concatenate([field, jnp.zeros_like(field)], axis=1)
+
+    rows = []
+    for picks in picked_tiles:
+        pieces = []
+        for k in range(0, K2, 2):
+            two = []
+            for q in (k, k + 1):
+                plane, at, same, use = picks[q]
+                both = table[plane, at]
+                kept = jnp.where(same, both, pltpu.roll(both, 64, 1))
+                two.append(jnp.where(use, kept, jnp.zeros_like(kept)))
+            pieces.append(jnp.where(lane8 < RANK, two[0], two[1]))
+        rows.append(jnp.concatenate(pieces, axis=1))
+    fields = mul_parts(jnp.concatenate(rows, axis=0), ca_high[...], ca_low[...], 1)
+    cf_out[...] = jnp.where(lane8 < RANK, 0.0, fields[8:])
+    for d in range(SUBS):
+        push(cf_out, cf_in.at[1, s], cf_send.at[1, d], cf_recv.at[1, d], (sibling, sub_at(d)))
+    cf_in[0, s] = jnp.where(lane8 < RANK, fields[:8], 0.0)
     for d in range(1, SUBS):
-        push(cf_all.at[s], cf_all.at[s], cf_send.at[d], cf_recv.at[d], (leaf, sub_at(d)))
-
-    for d in range(SUBS):
-        sub = lax.rem(s + SUBS - d, SUBS)
-        for i, part in enumerate((x_part, c_part)):
-            arrived(i, 1, d, part(2 - 2 * c, sub))
-            if d:
-                arrived(i, 2, d, part(2 * c, sub))
-    lane = lax.broadcasted_iota(jnp.int32, (ROWS, 128), 1)
-
-    def picked(entry, k, use):
-        both = ctab[lax.div(entry, 2)]
-        turned = pltpu.roll(both, 64, 1)
-        keep = jnp.where(lax.rem(entry, 2) == k % 2, 1.0, 0.0) * use
-        return both * keep + turned * (use - keep)
-
-    loads["la"].wait()
-    loads["near"].wait()
-    for j in range(4):
-        pieces = []
-        for k in range(0, KA, 2):
-            lo, hi = (
-                picked(leaf_list[j, q], q, jnp.where(q < leaf_count[j], 1.0, 0.0))
-                for q in (k, k + 1)
-            )
-            pieces.append(jnp.where(lane < RANK, lo, hi))
-        coupled = mul(jnp.concatenate(pieces, axis=1), la[j], 1)
-        far = mul(coupled, bases[j], 0)
-        sources = jnp.concatenate([xtab[near_list[j, k]] for k in range(NEAR)], axis=1)
-        pre[:, j * PTS : (j + 1) * PTS] = far + mul(sources, near[j], 1)
-
-    for d in range(1, SUBS):
-        slot = cf_all.at[lax.rem(s + SUBS - d, SUBS)]
-        remote(slot, slot, cf_send.at[d], cf_recv.at[d], (sibling, s)).wait_recv()
-    field_all = cf_all[...].reshape(ROWS, 128)[:, :RANK]
-    out_ref[...] = pre[...] + mul(field_all, mfold[...], 0)
+        push(cf_in.at[0, s], cf_in.at[0, s], cf_send.at[0, d], cf_recv.at[0, d], (leaf, sub_at(d)))
+
+    @pl.when(near_last)
+    def _():
+        near_field()
+
+    for cc in range(CORES):
+        for d in range(1 - cc, SUBS):
+            slot = cf_in.at[cc, lax.rem(s + SUBS - d, SUBS)]
+            remote(slot, slot, cf_send.at[cc, d], cf_recv.at[cc, d], (sibling, s)).wait_recv()
+    both = (cf_in[0] + cf_in[1]).reshape(ROWS, 128)
+    field_ref[...] = (both + pltpu.roll(both, 64, 1))[:, :RANK]
 
     for cp in sent:
         cp.wait_send()
@@ -406,11 +482,15 @@
     stay = functools.partial(pltpu.with_memory_space_constraint, memory_space=pltpu.HBM)
     in_hbm = pl.BlockSpec(memory_space=pltpu.HBM)
     dma = pltpu.SemaphoreType.DMA
-    return pl.pallas_call(
+    pre, fold, field = pl.pallas_call(
         kernel,
-        out_shape=jax.ShapeDtypeStruct(vectors.shape, F32),
+        out_shape=(
+            jax.ShapeDtypeStruct(vectors.shape, F32),
+            jax.ShapeDtypeStruct((RANK, 4 * PTS), F32),
+            jax.ShapeDtypeStruct((ROWS, RANK), F32),
+        ),
         in_specs=[in_hbm] * 12,
-        out_specs=pl.BlockSpec(memory_space=pltpu.VMEM),
+        out_specs=(pl.BlockSpec(memory_space=pltpu.VMEM),) * 3,
         scratch_shapes=[
             pltpu.SMEM(near_list.shape, jnp.int32),
             pltpu.SMEM(leaf_list.shape, jnp.int32),
@@ -425,13 +505,19 @@
             pltpu.VMEM(near_blocks.shape, F32),
             pltpu.VMEM(leaf_coupling.shape, F32),
             pltpu.VMEM(coarse_coupling.shape, F32),
-            pltpu.VMEM((RANK, 4 * PTS), F32),
-            pltpu.VMEM((ROWS, 4 * PTS), F32),
+            pltpu.VMEM(near_blocks.shape, BF16),
+            pltpu.VMEM(near_blocks.shape, BF16),
+            pltpu.VMEM((2 * RANK, K2 * RANK), BF16),
+            pltpu.VMEM((2 * RANK, K2 * RANK), BF16),
             pltpu.VMEM((SUBS, 8, 128), F32),
             pltpu.VMEM((SUBS, 2, 8, 128), F32),
             pltpu.VMEM((8, 128), F32),
             pltpu.VMEM((NZ, NY, 8, 128), F32),
-            pltpu.VMEM((SUBS, 8, 128), F32),
+            pltpu.VMEM((8, 128), F32),
+            pltpu.VMEM((CORES, SUBS, 8, 128), F32),
+            pltpu.VMEM(coarse_coupling.shape, F32),
+            pltpu.SMEM(coarse_list.shape, jnp.int32),
+            pltpu.SMEM(coarse_count.shape, jnp.int32),
             pltpu.SemaphoreType.REGULAR((NZ // 2,)),
             dma((15,)),
             dma((2, 3, SUBS)),
@@ -440,10 +526,10 @@
             dma((SUBS, 2)),
             dma((NZ // 2,)),
             dma((NZ // 2,)),
-            dma((NZ // 2,)),
-            dma((NZ // 2,)),
-            dma((SUBS,)),
-            dma((SUBS,)),
+            dma((3,)),
+            dma((3,)),
+            dma((CORES, SUBS)),
+            dma((CORES, SUBS)),
         ],
         compiler_params=pltpu.CompilerParams(
             collective_id=0, has_side_effects=True, vmem_limit_bytes=32 * 1024 * 1024
@@ -462,6 +548,7 @@
         stay(leaf_coupling),
         stay(coarse_coupling),
     )
+    return pre + jnp.dot(field, fold, precision=lax.Precision.HIGHEST)
 
 
 def solution(mesh):

time: 37.4 us -> 37.6 us (level)
  matrix products: 0 us -> 0.92 us
  local copies, waits for them, and re-layouts: 0.66 us -> 0 us
    dot_general x0 -> x1, matrix products: none -> 0.92 us  [per_device(): return pre + jnp.dot(field, fold, precision=lax.Precision.HIGHEST)]
    unnamed x1 -> x0, local copies, waits for them, and re-layouts: 0.66 us -> none
where the time goes in v5:
time: 37.6 us; the launch traced here: 37.5 us
  Pallas kernels  35.9 us (95%)
  matrix products  0.92 us (2%)
  between operations  0.66 us (2%)
    pallas_call x1, Pallas kernels, per_device(): pl.pallas_call(kernel, out_shape=(jax.ShapeDtypeStruct(vectors.shape, F32...  35.9 us
    dot_general x1, matrix products, per_device(): return pre + jnp.dot(field, fold, precision=lax.Precision.HIGHEST)  0.92 us

profile of v5, /device:TPU:1, one launch (start us, length us, event | category | flops | bytes accessed | tf_op | source)
XLA Modules:
  0.0 37.5 jit_solution(5311380747360405122)
XLA Ops:
  0.7 35.9 %shard_map.118 = (f32[32,1024]{1,0:T(8,128)S(1)}, f32[64,1024]{1,0:T(8,128)S(1)}, f32[32,64]{1,0:T(8,128)S(1)}) custom-call(s32[4,3]{1,0:T(4,128)} %near_list_hbm.1, s32[4,6]{1,0:T(4,128)} %leaf_list_hbm.1, s32[4]{0:T(128)} %leaf_count_hbm.1, s32[1,16]{1,0:T(1,128)} %coarse_list_hbm.1, s32[1]{0:T(128)S(6)} %copy.13.coarse_count_hbm, f32[32,1024]{1,0:T(8,128)} %x_hbm.1, ...), custom_call_target="tpu_custom_call" | custom-call | tf_op jit(solution)/shard_map/pallas_call | solution.py:485
  36.5 0.9 %convolution_add_fusion = f32[32,1024]{1,0:T(8,128)} fusion(f32[32,1024]{1,0:T(8,128)S(1)} %get-tuple-element.8, f32[32,64]{1,0:T(8,128)S(1)} %get-tuple-element.9, f32[64,1024]{1,0:T(8,128)S(1)} %get-tuple-element.10), kind=kOutput, calls=%fused_computation | convolution fusion | flops 25198592 | bytes 532480 | tf_op jit(solution)/shard_map/dot_general | solution.py:551
